TPU v7x, 32 devices: a whole 2x2x4 slice. The times are simulated.
32 devices in a mesh: row: 4 (over z), col: 8 (over y, x, core).
Axes of the slice: x: 2, y: 2, z: 4, core: 2. Of those that a mesh axis runs over, the one named last changes fastest.
Arguments:
- values: bfloat16 [32, 8, 128, 128], P('row', 'col'), may hold values from -0.375 to 0.375
- column_slot_index: int32 [32, 8], P('row', 'col'), may hold values from 0 to 3
- branches: int32 [2], replicated, may hold values from 0 to 1, as said below
Outputs:
- purified: bfloat16 [32, 8, 128, 128], P('row', 'col')
Inputs may be any that keep to these rules, and one draw needn't show every extreme that they name: column_slot_index[i, c] places block row i's single nonzero block among the 4 block columns of col index c. Branch 0 squares, branch 1 takes 2 X - X X; consecutive steps take different branches.
All inputs are finite; a program needn't handle non-finite values.
Results may differ from a plain program's by a relative error of at most 0.0051.
Values may be sent and summed in bfloat16 or wider, within the bound.
A program may use at most 64 MiB of HBM per device.

v0:
```python
import jax
import jax.numpy as jnp
from jax import lax
from jax.sharding import PartitionSpec as P

BPD = 4
STEPS = 2


def body(values, column_slot_index, branches):
    state = values
    own_ids = column_slot_index[:, 0]
    for step in range(STEPS):
        below, lower_block_index = (
            lax.all_gather(state, "row", axis=0, tiled=True),
            lax.all_gather(column_slot_index, "row", axis=0, tiled=True),
        )
        below_blocks = below[:, 0]
        below_pos = lower_block_index[:, 0]
        block_strip, panel_ids = (
            lax.all_gather(state, "col", axis=1, tiled=True),
            lax.all_gather(column_slot_index, "col", axis=1, tiled=True),
        )
        count = block_strip.shape[1]
        slots = jnp.arange(count, dtype=jnp.int32)
        desired_trace = slots[None, :] * BPD + panel_ids
        selected_blocks = jnp.take(below_blocks, desired_trace, axis=0)
        match = jnp.take(below_pos, desired_trace, axis=0) == own_ids[:, None]
        selected_blocks = jnp.where(
            match[:, :, None, None], selected_blocks, jnp.zeros_like(selected_blocks)
        )
        matrix_square = jnp.einsum(
            "jlut,jlto->juo", block_strip, selected_blocks, preferred_element_type=jnp.float32
        )
        twice_density = 2.0 * state[:, 0].astype(jnp.float32) - matrix_square
        newer = jnp.where(branches[step] == 1, twice_density, matrix_square)
        state = newer.astype(jnp.bfloat16)[:, None]
    return state


def solution(mesh):
    in_specs = (P("row", "col", None, None), P("row", "col"), P())
    out_specs = P("row", "col", None, None)
    return jax.shard_map(body, mesh=mesh, in_specs=in_specs, out_specs=out_specs, check_vma=False)
```

profile of v0, /device:TPU:0, one launch (start us, length us, event | category | flops | bytes accessed | tf_op | source)
XLA Modules:
  0.0 146.5 jit_solution(17894452063335819616)
XLA Ops:
  6.5 0.0 all-gather.8.cloned.1.call-start
  6.5 0.7 all-gather.8.cloned.1.call-update
  7.3 0.0 all-gather.10.cloned.1.call-start
  7.3 0.7 all-gather.10.cloned.1.call-update
  8.0 0.0 all-gather.14.cloned.1.call-start
  8.1 1.1 copy.32
  9.2 10.3 %all-gather.2 = s32[8,1,8]{2,1,0:T(1,128)S(1)} all-gather(s32[1,1,8]{2,1,0:T(1,128)} %bitcast.52), channel_id=1, replica_groups=mesh['row'=4,'col'=8] {'col'}, dimensions={0}, use_global_device_ids=true | all-gather | bytes 288 | tf_op jit(solution)/shard_map/all_gather | solution.py:22
  19.5 0.1 compare_select_fusion
  19.6 0.1 copy.33
  19.6 0.1 reshape.66
  19.7 1.2 dynamic-slice
  21.6 0.8 bitcast_dynamic-update-slice_fusion
  22.4 8.7 %all-reduce = s32[32]{0:T(128)S(1)} all-reduce(s32[32]{0:T(128)S(1)} %bitcast_dynamic-update-slice_fusion), channel_id=1, replica_groups=mesh['row'=4,'col'=8] {'row'}, use_global_device_ids=true, to_apply=%add | all-reduce | flops 32 | bytes 256 | tf_op jit(solution)/shard_map/squeeze | solution.py:19
  31.1 0.0 copy-start.2
  31.1 0.0 copy-start.3
  31.1 0.8 gather_fusion
  31.9 0.1 reshape.69
  32.0 0.1 copy.34
  32.0 0.0 copy-done.2
  32.0 0.1 select_compare_fusion
  32.1 0.1 copy.36
  32.2 0.1 copy.35
  32.3 0.0 copy-done.3
  32.3 0.6 fusion.37
  33.5 6.2 %all-gather.8.cloned.1.call-done = bf16[32,1,128,128]{3,2,1,0:T(8,128)(2,1)} async-done(((bf16[8,1,128,128]{3,2,1,0:T(8,128)(2,1)}), bf16[32,1,128,128]{3,2,1,0:T(8,128)(2,1)}) %all-gather.8.cloned.1.call-update) | async-done | bytes 1048592 | tf_op jit(solution)/shard_map/all_gather | solution.py:15
  39.8 2.2 %gather_fusion.1 = bf16[64,128,128]{2,1,0:T(8,128)(2,1)S(1)} fusion(bf16[32,128,128]{2,1,0:T(8,128)(2,1)} %bitcast.45, s32[1024]{0:T(1024)S(1)} %pad_clamp_fusion), kind=kCustom, calls=%fused_computation.1.clone | custom fusion | bytes 4194560 | tf_op jit(solution)/shard_map/jit(_take)/gather | solution.py:27
  41.9 27.1 %all-gather.10.cloned.1.call-done = bf16[8,8,128,128]{3,2,1,0:T(8,128)(2,1)} async-done(((bf16[8,1,128,128]{3,2,1,0:T(8,128)(2,1)}), bf16[8,8,128,128]{3,2,1,0:T(8,128)(2,1)}) %all-gather.10.cloned.1.call-update) | async-done | bytes 2097168 | tf_op jit(solution)/shard_map/all_gather | solution.py:21
  69.1 4.1 %copy.48 = bf16[8,8,128,128]{2,1,3,0:T(8,128)(2,1)} copy(bf16[8,8,128,128]{3,2,1,0:T(8,128)(2,1)} %all-gather.10.cloned.1.call-done) | data formatting | bytes 4194304 | tf_op jit(solution)/shard_map/all_gather | solution.py:21
  73.2 3.4 %fusion.30 = bf16[8,128,128]{1,2,0:T(8,128)(2,1)S(1)} fusion(bf16[8,8,128,128]{2,1,3,0:T(8,128)(2,1)} %copy.48, bf16[8,8,128,128]{3,2,1,0:T(8,128)(2,1)S(1)} %bitcast.47, pred[8,8]{1,0:T(8,128)(4,1)S(1)} %copy.36, pred[8,8]{1,0:T(8,128)(4,1)S(1)} %copy.35, bf16[8,1,128,128]{2,3,0,1:T(8,128)(2,1)S(1)} %copy.32, pred[]{:T(512)} %bitcast.1), kind=kOutput, calls=%fused_computation.23 | convolution fusion | flops 271187968 | bytes 4718721 | tf_op jit(solution)/shard_map/jlut,jlto->juo/dot_general | solution.py:32
  76.6 0.0 copy-start
  76.6 0.9 copy.41
  77.5 0.0 all-gather.14.cloned.1.call-update
  77.5 0.0 all-gather.12.cloned.1.call-start
  77.5 0.0 copy-done
  77.5 0.5 all-gather.12.cloned.1.call-update
  78.6 26.9 %all-gather.14.cloned.1.call-done = bf16[32,128,128]{2,1,0:T(8,128)(2,1)} async-done(((bf16[8,128,128]{2,1,0:T(8,128)(2,1)}), bf16[32,128,128]{2,1,0:T(8,128)(2,1)}) %all-gather.14.cloned.1.call-update) | async-done | bytes 1048592 | tf_op jit(solution)/shard_map/all_gather | solution.py:15
  105.6 2.2 %gather_fusion.2 = bf16[64,128,128]{2,1,0:T(8,128)(2,1)S(1)} fusion(bf16[32,128,128]{2,1,0:T(8,128)(2,1)} %all-gather.14.cloned.1.call-done, s32[1024]{0:T(1024)S(1)} %pad_clamp_fusion), kind=kCustom, calls=%fused_computation.2.clone | custom fusion | bytes 4194560 | tf_op jit(solution)/shard_map/jit(_take)/gather | solution.py:27
  107.8 27.3 %all-gather.12.cloned.1.call-done = bf16[8,1024,128]{1,2,0:T(8,128)(2,1)} async-done(((bf16[8,128,128]{1,2,0:T(8,128)(2,1)}), bf16[8,1024,128]{1,2,0:T(8,128)(2,1)}) %all-gather.12.cloned.1.call-update) | async-done | bytes 2097168 | tf_op jit(solution)/shard_map/all_gather | solution.py:21
  135.0 0.0 copy-start.1
  135.0 2.3 %copy.53 = bf16[128,8,8,128]{3,2,1,0:T(8,128)(2,1)S(1)} copy(bf16[128,8,8,128]{3,1,2,0:T(8,128)(2,1)} %bitcast.48) | data formatting | bytes 4194304
  137.3 0.0 copy-done.1
  137.3 1.8 %fusion.25 = bf16[8,1,128,128]{2,3,0,1:T(8,128)(2,1)S(1)} fusion(bf16[8,8,128,128]{2,1,3,0:T(8,128)(2,1)S(1)} %bitcast.49, bf16[8,8,128,128]{3,2,1,0:T(8,128)(2,1)S(1)} %bitcast.46, pred[8,8]{1,0:T(8,128)(4,1)S(1)} %copy.36, pred[8,8]{1,0:T(8,128)(4,1)S(1)} %copy.35, bf16[8,128,128]{1,2,0:T(8,128)(2,1)S(1)} %copy-done.1, pred[]{:T(512)} %bitcast), kind=kOutput, calls=%fused_computation.21 | convolution fusion | flops 271187968 | bytes 4718721 | tf_op jit(solution)/shard_map/jlut,jlto->juo/dot_general | solution.py:32
  139.1 0.9 copy.46
  (3 shorter events, 0.0 us)
Async XLA Ops:
  6.5 33.2 %all-gather.8.cloned.1.call-start = ((), (), s32[]{:S(2)}) async-start(), calls=%async_computation | async-start | bytes 1310720 | tf_op jit(solution)/shard_map/all_gather | solution.py:15
  7.3 61.8 %all-gather.10.cloned.1.call-start = ((), (), s32[]{:S(2)}) async-start(), calls=%async_computation.1 | async-start | bytes 2359296 | tf_op jit(solution)/shard_map/all_gather | solution.py:21
  8.0 97.6 %all-gather.14.cloned.1.call-start = ((), (), s32[]{:S(2)}) async-start(), calls=%async_computation.3 | async-start | bytes 1310720 | tf_op jit(solution)/shard_map/all_gather | solution.py:15
  31.1 1.0 copy-start.2
  31.1 1.2 copy-start.3
  76.6 0.9 copy-start
  77.5 57.5 %all-gather.12.cloned.1.call-start = ((), (), s32[]{:S(2)}) async-start(), calls=%async_computation.2 | async-start | bytes 2359296 | tf_op jit(solution)/shard_map/all_gather | solution.py:21
  135.0 2.3 %copy-start.1 = (bf16[8,128,128]{1,2,0:T(8,128)(2,1)S(1)}, bf16[8,128,128]{1,2,0:T(8,128)(2,1)}, u32[]{:S(2)}) copy-start(bf16[8,128,128]{1,2,0:T(8,128)(2,1)} %copy-done) | copy-start | bytes 786436
Sparse Core Ops, SparseCore 0:
  8.9 30.7 all-gather.7
  41.7 27.3 all-gather.9
  77.6 27.9 all-gather.13
  107.3 27.6 all-gather.11
where the time goes:
time: 147 us; the launch traced here: 146 us
  waiting for transfers between devices  89.5 us (61%)
  blocking collectives  19 us (13%)
  local copies, waits for them, and re-layouts  17.4 us (12%)
  between operations  15.1 us (10%)
  matrix products  5.19 us (4%)
    all_gather x2, waiting for transfers between devices, body(): lax.all_gather(state, 'col', axis=1, tiled=True)  54.4 us
    all_gather x2, waiting for transfers between devices, body(): lax.all_gather(state, 'row', axis=0, tiled=True)  33.2 us
    all_gather x1, blocking collectives, body(): lax.all_gather(column_slot_index, 'col', axis=1, tiled=True)  10.3 us
    squeeze x1, blocking collectives, body(): below_pos = lower_block_index[:, 0]  8.69 us
    unnamed x13, local copies, waits for them, and re-layouts  5.39 us
    dot_general x2, matrix products, body(): jnp.einsum('jlut,jlto->juo', block_strip, selected_blocks, preferred_elem...  5.19 us
    gather x2, local copies, waits for them, and re-layouts, body(): selected_blocks = jnp.take(below_blocks, desired_trace, axis=0)  4.35 us
    all_gather x1, local copies, waits for them, and re-layouts, body(): lax.all_gather(state, 'col', axis=1, tiled=True)  4.09 us
  transfers between devices with their start and end apart: 4, of which 4 were waited for; matrix products, arithmetic and copies ran while one was open for 6% of the time, Pallas kernels for 0%

commit v1 on v0

v1 whole, which is shorter than its diff:
```python
import functools

import jax
import jax.numpy as jnp
from jax import lax
from jax.experimental import pallas as pl
from jax.experimental.pallas import tpu as pltpu
from jax.sharding import PartitionSpec as P

BPD = 4
MESH = pl.DeviceIdType.MESH


def flip(index, bits):
    out, place = index, 1
    while place <= bits:
        if bits & place:
            out = out + place - 2 * place * lax.rem(lax.div(index, place), 2)
        place *= 2
    return out


def kernel(n, ncol, steps, branches, values, ids, out, *scratch):
    rows = values.shape[0]
    per = rows // BPD
    chips = ncol // 2
    bufs = [scratch[s * n:(s + 1) * n] for s in range(steps)]
    scratch = scratch[steps * n:]
    strips, scratch = scratch[:steps], scratch[steps:]
    (acc, own_ids, col_ids, strip_ids, col_s, strip_s,
     id_send, id_recv_z, id_recv_c, local_sem,
     z_send, z_recv, c_send, p_send, c_recv) = scratch

    z, c = lax.axis_index("row"), lax.axis_index("col")
    chip, core = lax.div(c, 2), lax.rem(c, 2)
    peer = c + 1 - 2 * core

    col_others = [lax.rem(c + j, ncol) for j in range(1, ncol)]
    row_others = [lax.rem(z + j, n) for j in range(1, n)]
    barrier = pltpu.get_barrier_semaphore()
    for other in col_others:
        pl.semaphore_signal(barrier, inc=1, device_id=(z, other), device_id_type=MESH)
    for other in row_others:
        pl.semaphore_signal(barrier, inc=1, device_id=(other, c), device_id_type=MESH)
    own_ids[...] = jnp.zeros_like(own_ids)
    own_ids[0:rows, :] = jnp.broadcast_to(ids[...], (rows, own_ids.shape[1]))
    pl.semaphore_wait(barrier, ncol + n - 2)

    def remote(src, dst, send, recv, device):
        return pltpu.make_async_remote_copy(
            src_ref=src, dst_ref=dst, send_sem=send, recv_sem=recv,
            device_id=device, device_id_type=MESH)

    def z_copy(step, d, down):
        src = values if step == 0 and d == 0 else bufs[step][d]
        at = d + 1 if down else (d - 1) % n
        return remote(
            src.at[0:rows], bufs[step][at % n].at[0:rows],
            z_send.at[step, 0 if down else 1, d], z_recv.at[step, at % n],
            (jnp.maximum(z - 1, 0) if down else jnp.minimum(z + 1, n - 1), c))

    def z_arrival(step, d):
        return remote(
            bufs[step][d].at[0:rows], bufs[step][d].at[0:rows],
            z_send.at[step, 0, d], z_recv.at[step, d], (z, peer))

    def c_copy(step, j):
        src = values.at[0:rows] if step == 0 else bufs[step][0].at[0:rows]
        return remote(src, strips[step].at[c], c_send.at[step, j], c_recv.at[step, c],
                      (z, flip(chip, j) * 2 + core if j else peer))

    def p_copy(step, j):
        origin = flip(chip, j) * 2 + core
        return remote(strips[step].at[origin], strips[step].at[origin],
                      p_send.at[step, j], c_recv.at[step, origin], (z, peer))

    def c_arrival(step, origin):
        return remote(strips[step].at[origin], strips[step].at[origin],
                      p_send.at[step, 0], c_recv.at[step, origin], (z, peer))

    def send_own(step):
        @pl.when(z > 0)
        def _():
            z_copy(step, 0, True).start()

        @pl.when(z < n - 1)
        def _():
            z_copy(step, 0, False).start()

        for j in list(range(1, chips)) + [0]:
            c_copy(step, j).start()

    def add(step, d, q):
        for i in range(rows):
            left, right = [], []
            for t in range(per):
                p = q * per + t
                slot = strip_s[p, i, 0]
                k = t * BPD + slot
                k = jnp.where(col_s[q, k, 0] == col_s[z, i, 0], k, rows)
                left.append(strips[step][p, i])
                right.append(bufs[step][d][k])
            term = jnp.dot(jnp.concatenate(left, 1), jnp.concatenate(right, 0),
                           preferred_element_type=jnp.float32)
            acc[i] = term if d == 0 else acc[i] + term

    sent_ids = []
    for t, other in enumerate(col_others):
        sent_ids.append(remote(own_ids, strip_ids.at[c], id_send.at[t], id_recv_c.at[c], (z, other)))
    for t, other in enumerate(row_others):
        sent_ids.append(remote(own_ids, col_ids.at[z], id_send.at[ncol - 1 + t], id_recv_z.at[z], (other, c)))
    send_own(0)
    for copy in sent_ids:
        copy.start()
    bufs[0][0][0:rows] = values[...]
    strips[0][c] = values[...]
    strip_ids[c] = own_ids[...]
    col_ids[z] = own_ids[...]
    for step in range(steps):
        for d in range(n):
            bufs[step][d][rows] = jnp.zeros(values.shape[1:], values.dtype)
    for other in col_others:
        remote(own_ids, strip_ids.at[other], id_send.at[0], id_recv_c.at[other], (z, other)).wait_recv()
    for other in row_others:
        remote(own_ids, col_ids.at[other], id_send.at[0], id_recv_z.at[other], (other, c)).wait_recv()
    to_strip = pltpu.make_async_copy(strip_ids, strip_s, local_sem.at[0])
    to_col = pltpu.make_async_copy(col_ids, col_s, local_sem.at[1])
    to_strip.start()
    to_col.start()
    to_strip.wait()
    to_col.wait()

    for step in range(steps):
        def take(m):
            @pl.when(z + m < n)
            def _():
                z_arrival(step, m).wait_recv()
                if m + 1 < n:
                    @pl.when(z > 0)
                    def _():
                        z_copy(step, m, True).start()

            @pl.when(z - m >= 0)
            def _():
                z_arrival(step, n - m).wait_recv()
                if m + 1 < n:
                    @pl.when(z < n - 1)
                    def _():
                        z_copy(step, n - m, False).start()

        def use(m):
            if m == 0:
                add(step, 0, z)
                return

            @pl.when(z + m < n)
            def _():
                add(step, m, z + m)

            @pl.when(z - m >= 0)
            def _():
                add(step, n - m, z - m)

        def take_col(js):
            for j in js:
                c_arrival(step, flip(chip, j) * 2 + core).wait_recv()
                p_copy(step, j).start()

        done = 0
        for m in range(1, n):
            take(m)
            if m == 1:
                take_col(range(1, min(3, chips)))
            if m == min(2, n - 1):
                take_col(range(3, chips))
                for j in range(chips):
                    c_arrival(step, flip(chip, j) * 2 + 1 - core).wait_recv()
                use(0)
                done = 1
            if done:
                while done < m:
                    use(done)
                    done += 1
        while done < n:
            use(done)
            done += 1

        branch = branches[step]
        for i in range(rows):
            old = bufs[step][0][i].astype(jnp.float32)
            total = acc[i]
            new = jnp.where(branch == 1, 2.0 * old - total, total).astype(values.dtype)
            if step == steps - 1:
                out[i] = new
            else:
                bufs[step + 1][0][i] = new
                strips[step + 1][c, i] = new
        if step < steps - 1:
            send_own(step + 1)

    for copy in sent_ids:
        copy.wait_send()
    for step in range(steps):
        for j in range(chips):
            c_copy(step, j).wait_send()
            if j:
                p_copy(step, j).wait_send()
        for d in range(n - 1):
            @pl.when((z > 0) & (z + d < n))
            def _():
                z_copy(step, d, True).wait_send()

            @pl.when((z < n - 1) & (z - d >= 0))
            def _():
                z_copy(step, (n - d) % n, False).wait_send()


def purify(n, ncol, values, column_slot_index, branches):
    rows, _, bs, _ = values.shape
    steps = branches.shape[0]
    block = (rows, bs, bs)
    id_rows = -(-rows // 8) * 8
    scratch = [pltpu.VMEM((rows + 1, bs, bs), values.dtype) for _ in range(steps * n)]
    scratch += [pltpu.VMEM((ncol,) + block, values.dtype) for _ in range(steps)]
    scratch += [
        pltpu.VMEM(block, jnp.float32),
        pltpu.VMEM((id_rows, 128), jnp.int32),
        pltpu.VMEM((n, id_rows, 128), jnp.int32),
        pltpu.VMEM((ncol, id_rows, 128), jnp.int32),
        pltpu.SMEM((n, id_rows, 128), jnp.int32),
        pltpu.SMEM((ncol, id_rows, 128), jnp.int32),
        pltpu.SemaphoreType.DMA((ncol + n - 2,)),
        pltpu.SemaphoreType.DMA((n,)),
        pltpu.SemaphoreType.DMA((ncol,)),
        pltpu.SemaphoreType.DMA((2,)),
        pltpu.SemaphoreType.DMA((steps, 2, n)),
        pltpu.SemaphoreType.DMA((steps, n)),
        pltpu.SemaphoreType.DMA((steps, ncol // 2)),
        pltpu.SemaphoreType.DMA((steps, ncol // 2)),
        pltpu.SemaphoreType.DMA((steps, ncol)),
    ]
    vmem = pl.BlockSpec(memory_space=pltpu.VMEM)
    new = pl.pallas_call(
        functools.partial(kernel, n, ncol, steps),
        out_shape=jax.ShapeDtypeStruct(block, values.dtype),
        in_specs=[pl.BlockSpec(memory_space=pltpu.SMEM), vmem, vmem],
        out_specs=vmem,
        scratch_shapes=scratch,
        compiler_params=pltpu.CompilerParams(
            collective_id=0, has_side_effects=True, vmem_limit_bytes=48 * 2**20),
    )(branches, values.reshape(block), column_slot_index)
    return new.reshape(values.shape)


def solution(mesh):
    in_specs = (P("row", "col", None, None), P("row", "col"), P())
    out_specs = P("row", "col", None, None)
    body = functools.partial(purify, mesh.shape["row"], mesh.shape["col"])
    return jax.shard_map(body, mesh=mesh, in_specs=in_specs, out_specs=out_specs, check_vma=False)
```

time: 147 us -> 58 us (0.39)
  waiting for transfers between devices: 89.5 us -> 0 us
  Pallas kernels: 0 us -> 54.8 us
  blocking collectives: 19 us -> 0 us
  between operations: 15.1 us -> 0.01 us
  local copies, waits for them, and re-layouts: 17.4 us -> 2.96 us
  matrix products: 5.19 us -> 0 us
    all_gather x4 -> x0, waiting for transfers between devices: 87.6 us -> none  [the longest x2 54.4 us: body(): lax.all_gather(state, 'col', axis=1, tiled=True)]
    pallas_call x0 -> x1, Pallas kernels: none -> 54.8 us  [purify(): pl.pallas_call(functools.partial(kernel, n, ncol, steps), out_shape=jax.S...]
    all_gather x1 -> x0, blocking collectives: 10.3 us -> none  [body(): lax.all_gather(column_slot_index, 'col', axis=1, tiled=True)]
    squeeze x1 -> x0, blocking collectives: 8.69 us -> none  [body(): below_pos = lower_block_index[:, 0]]
    gather x5 -> x0, local copies, waits for them, and re-layouts: 5.27 us -> none  [the longest x2 4.35 us: body(): selected_blocks = jnp.take(below_blocks, desired_trace, axis=0)]
    dot_general x2 -> x0, matrix products: 5.19 us -> none  [body(): jnp.einsum('jlut,jlto->juo', block_strip, selected_blocks, preferred_elem...]
    all_gather x1 -> x0, local copies, waits for them, and re-layouts: 4.09 us -> none  [body(): lax.all_gather(state, 'col', axis=1, tiled=True)]
    unnamed x13 -> x8, local copies, waits for them, and re-layouts: 5.39 us -> 2.96 us
  transfers between devices with their start and end apart: 4 -> 0, of which waited for: 4 -> 0; matrix products, arithmetic and copies ran while one was open for 6% -> 0% of each run, Pallas kernels for 0% -> 0%
where the time goes in v1:
time: 58 us; the launch traced here: 57.8 us
  Pallas kernels  54.8 us (94%)
  local copies, waits for them, and re-layouts  2.96 us (5%)
    pallas_call x1, Pallas kernels, purify(): pl.pallas_call(functools.partial(kernel, n, ncol, steps), out_shape=jax.S...  54.8 us
    unnamed x8, local copies, waits for them, and re-layouts  2.96 us

profile of v1, /device:TPU:0, one launch (start us, length us, event | category | flops | bytes accessed | tf_op | source)
XLA Modules:
  0.0 57.8 jit_solution(10861595072044431790)
XLA Ops:
  0.0 0.0 copy-start.2
  0.0 0.7 %copy-done.2 = s32[8,1]{0,1:T(1,128)S(1)} copy-done((s32[8,1]{0,1:T(1,128)S(1)}, s32[8,1]{0,1:T(1,128)}, u32[]{:S(2)}) %copy-start.2) | copy-done | bytes 56
  0.7 0.0 copy-start.1
  0.7 0.1 copy.4.ids
  0.7 0.6 copy-done.1
  1.3 0.0 copy-start
  1.3 0.9 %copy-done = bf16[8,1,128,128]{3,2,1,0:T(8,128)(2,1)S(1)} copy-done((bf16[8,1,128,128]{3,2,1,0:T(8,128)(2,1)S(1)}, bf16[8,1,128,128]{3,2,1,0:T(8,128)(2,1)}, u32[]{:S(2)}) %copy-start) | copy-done | bytes 262168
  2.3 54.8 %shard_map.37 = bf16[8,128,128]{2,1,0:T(8,128)(2,1)S(1)} custom-call(s32[2]{0:T(128)S(1)} %copy-done.1, bf16[8,128,128]{2,1,0:T(8,128)(2,1)S(1)} %bitcast.5, s32[8,1]{1,0:T(8,128)S(1)} %copy.4.ids), custom_call_target="tpu_custom_call" | custom-call | tf_op jit(solution)/shard_map/pallas_call | solution.py:243
  57.1 0.7 %copy.7 = bf16[8,1,128,128]{3,2,1,0:T(8,128)(2,1)} copy(bf16[8,1,128,128]{3,2,1,0:T(8,128)(2,1)S(1)} %bitcast.4) | data formatting | bytes 524288
Async XLA Ops:
  0.0 0.7 %copy-start.2 = (s32[8,1]{0,1:T(1,128)S(1)}, s32[8,1]{0,1:T(1,128)}, u32[]{:S(2)}) copy-start(s32[8,1]{0,1:T(1,128)} %param.4) | copy-start | bytes 100
  0.7 0.7 %copy-start.1 = (s32[2]{0:T(128)S(1)}, s32[2]{0:T(128)}, u32[]{:S(2)}) copy-start(s32[2]{0:T(128)} %branches.1) | copy-start | bytes 28
  1.3 0.9 %copy-start = (bf16[8,1,128,128]{3,2,1,0:T(8,128)(2,1)S(1)}, bf16[8,1,128,128]{3,2,1,0:T(8,128)(2,1)}, u32[]{:S(2)}) copy-start(bf16[8,1,128,128]{3,2,1,0:T(8,128)(2,1)} %param.3) | copy-start | bytes 786436

commit v2 on v1

--- a/solution.py
+++ b/solution.py
@@ -8,6 +8,7 @@
 from jax.sharding import PartitionSpec as P
 
 BPD = 4
+PIECES = 4
 MESH = pl.DeviceIdType.MESH
 
 
@@ -23,11 +24,12 @@
 def kernel(n, ncol, steps, branches, values, ids, out, *scratch):
     rows = values.shape[0]
     per = rows // BPD
+    part = rows // PIECES
     chips = ncol // 2
     bufs = [scratch[s * n:(s + 1) * n] for s in range(steps)]
     scratch = scratch[steps * n:]
     strips, scratch = scratch[:steps], scratch[steps:]
-    (acc, own_ids, col_ids, strip_ids, col_s, strip_s,
+    (acc, ids_in, branch_s, own_ids, col_ids, strip_ids, col_s, strip_s,
      id_send, id_recv_z, id_recv_c, local_sem,
      z_send, z_recv, c_send, p_send, c_recv) = scratch
 
@@ -35,6 +37,14 @@
     chip, core = lax.div(c, 2), lax.rem(c, 2)
     peer = c + 1 - 2 * core
 
+    loads = [
+        pltpu.make_async_copy(values, bufs[0][0].at[0:rows], local_sem.at[0]),
+        pltpu.make_async_copy(values, strips[0].at[c], local_sem.at[1]),
+        pltpu.make_async_copy(ids, ids_in, local_sem.at[2]),
+        pltpu.make_async_copy(branches, branch_s, local_sem.at[3]),
+    ]
+    for load in loads:
+        load.start()
     col_others = [lax.rem(c + j, ncol) for j in range(1, ncol)]
     row_others = [lax.rem(z + j, n) for j in range(1, n)]
     barrier = pltpu.get_barrier_semaphore()
@@ -43,7 +53,14 @@
     for other in row_others:
         pl.semaphore_signal(barrier, inc=1, device_id=(other, c), device_id_type=MESH)
     own_ids[...] = jnp.zeros_like(own_ids)
-    own_ids[0:rows, :] = jnp.broadcast_to(ids[...], (rows, own_ids.shape[1]))
+    for step in range(steps):
+        for d in range(n):
+            bufs[step][d][rows] = jnp.zeros(values.shape[1:], values.dtype)
+    for load in loads:
+        load.wait()
+    own_ids[0:rows, :] = jnp.broadcast_to(ids_in[...], (rows, own_ids.shape[1]))
+    strip_ids[c] = own_ids[...]
+    col_ids[z] = own_ids[...]
     pl.semaphore_wait(barrier, ncol + n - 2)
 
     def remote(src, dst, send, recv, device):
@@ -51,21 +68,22 @@
             src_ref=src, dst_ref=dst, send_sem=send, recv_sem=recv,
             device_id=device, device_id_type=MESH)
 
-    def z_copy(step, d, down):
-        src = values if step == 0 and d == 0 else bufs[step][d]
+    def z_copy(step, d, down, piece):
         at = d + 1 if down else (d - 1) % n
+        span = pl.ds(piece * part, part)
         return remote(
-            src.at[0:rows], bufs[step][at % n].at[0:rows],
-            z_send.at[step, 0 if down else 1, d], z_recv.at[step, at % n],
+            bufs[step][d].at[span], bufs[step][at].at[span],
+            z_send.at[step, 0 if down else 1, d, piece], z_recv.at[step, at, piece],
             (jnp.maximum(z - 1, 0) if down else jnp.minimum(z + 1, n - 1), c))
 
-    def z_arrival(step, d):
+    def z_arrival(step, d, piece):
+        span = pl.ds(piece * part, part)
         return remote(
-            bufs[step][d].at[0:rows], bufs[step][d].at[0:rows],
-            z_send.at[step, 0, d], z_recv.at[step, d], (z, peer))
+            bufs[step][d].at[span], bufs[step][d].at[span],
+            z_send.at[step, 0, d, piece], z_recv.at[step, d, piece], (z, peer))
 
     def c_copy(step, j):
-        src = values.at[0:rows] if step == 0 else bufs[step][0].at[0:rows]
+        src = bufs[step][0].at[0:rows]
         return remote(src, strips[step].at[c], c_send.at[step, j], c_recv.at[step, c],
                       (z, flip(chip, j) * 2 + core if j else peer))
 
@@ -78,17 +96,21 @@
         return remote(strips[step].at[origin], strips[step].at[origin],
                       p_send.at[step, 0], c_recv.at[step, origin], (z, peer))
 
-    def send_own(step):
+    def send_own(step, piece):
         @pl.when(z > 0)
         def _():
-            z_copy(step, 0, True).start()
+            z_copy(step, 0, True, piece).start()
 
         @pl.when(z < n - 1)
         def _():
-            z_copy(step, 0, False).start()
-
-        for j in list(range(1, chips)) + [0]:
+            z_copy(step, 0, False, piece).start()
+
+    def send_col(step, js):
+        for j in js:
             c_copy(step, j).start()
+
+    near = list(range(1, min(3, chips))) + [0]
+    far = list(range(3, chips))
 
     def add(step, d, q):
         for i in range(rows):
@@ -109,44 +131,41 @@
         sent_ids.append(remote(own_ids, strip_ids.at[c], id_send.at[t], id_recv_c.at[c], (z, other)))
     for t, other in enumerate(row_others):
         sent_ids.append(remote(own_ids, col_ids.at[z], id_send.at[ncol - 1 + t], id_recv_z.at[z], (other, c)))
-    send_own(0)
     for copy in sent_ids:
         copy.start()
-    bufs[0][0][0:rows] = values[...]
-    strips[0][c] = values[...]
-    strip_ids[c] = own_ids[...]
-    col_ids[z] = own_ids[...]
+    for piece in range(PIECES):
+        send_own(0, piece)
+    send_col(0, near)
+
+    def take_ids():
+        for other in col_others:
+            remote(own_ids, strip_ids.at[other], id_send.at[0], id_recv_c.at[other], (z, other)).wait_recv()
+        for other in row_others:
+            remote(own_ids, col_ids.at[other], id_send.at[0], id_recv_z.at[other], (other, c)).wait_recv()
+        to_strip = pltpu.make_async_copy(strip_ids, strip_s, local_sem.at[0])
+        to_col = pltpu.make_async_copy(col_ids, col_s, local_sem.at[1])
+        to_strip.start()
+        to_col.start()
+        to_strip.wait()
+        to_col.wait()
+
     for step in range(steps):
-        for d in range(n):
-            bufs[step][d][rows] = jnp.zeros(values.shape[1:], values.dtype)
-    for other in col_others:
-        remote(own_ids, strip_ids.at[other], id_send.at[0], id_recv_c.at[other], (z, other)).wait_recv()
-    for other in row_others:
-        remote(own_ids, col_ids.at[other], id_send.at[0], id_recv_z.at[other], (other, c)).wait_recv()
-    to_strip = pltpu.make_async_copy(strip_ids, strip_s, local_sem.at[0])
-    to_col = pltpu.make_async_copy(col_ids, col_s, local_sem.at[1])
-    to_strip.start()
-    to_col.start()
-    to_strip.wait()
-    to_col.wait()
-
-    for step in range(steps):
-        def take(m):
+        def take(m, piece):
             @pl.when(z + m < n)
             def _():
-                z_arrival(step, m).wait_recv()
+                z_arrival(step, m, piece).wait_recv()
                 if m + 1 < n:
                     @pl.when(z > 0)
                     def _():
-                        z_copy(step, m, True).start()
+                        z_copy(step, m, True, piece).start()
 
             @pl.when(z - m >= 0)
             def _():
-                z_arrival(step, n - m).wait_recv()
+                z_arrival(step, n - m, piece).wait_recv()
                 if m + 1 < n:
                     @pl.when(z < n - 1)
                     def _():
-                        z_copy(step, n - m, False).start()
+                        z_copy(step, n - m, False, piece).start()
 
         def use(m):
             if m == 0:
@@ -168,11 +187,15 @@
 
         done = 0
         for m in range(1, n):
-            take(m)
+            for piece in range(PIECES):
+                take(m, piece)
             if m == 1:
-                take_col(range(1, min(3, chips)))
+                send_col(step, far)
+                take_col(near[:-1])
             if m == min(2, n - 1):
-                take_col(range(3, chips))
+                take_col(far)
+                if step == 0:
+                    take_ids()
                 for j in range(chips):
                     c_arrival(step, flip(chip, j) * 2 + 1 - core).wait_recv()
                 use(0)
@@ -185,7 +208,7 @@
             use(done)
             done += 1
 
-        branch = branches[step]
+        branch = branch_s[step]
         for i in range(rows):
             old = bufs[step][0][i].astype(jnp.float32)
             total = acc[i]
@@ -195,8 +218,10 @@
             else:
                 bufs[step + 1][0][i] = new
                 strips[step + 1][c, i] = new
+                if (i + 1) % part == 0:
+                    send_own(step + 1, i // part)
         if step < steps - 1:
-            send_own(step + 1)
+            send_col(step + 1, near)
 
     for copy in sent_ids:
         copy.wait_send()
@@ -206,13 +231,14 @@
             if j:
                 p_copy(step, j).wait_send()
         for d in range(n - 1):
-            @pl.when((z > 0) & (z + d < n))
-            def _():
-                z_copy(step, d, True).wait_send()
-
-            @pl.when((z < n - 1) & (z - d >= 0))
-            def _():
-                z_copy(step, (n - d) % n, False).wait_send()
+            for piece in range(PIECES):
+                @pl.when((z > 0) & (z + d < n))
+                def _():
+                    z_copy(step, d, True, piece).wait_send()
+
+                @pl.when((z < n - 1) & (z - d >= 0))
+                def _():
+                    z_copy(step, (n - d) % n, False, piece).wait_send()
 
 
 def purify(n, ncol, values, column_slot_index, branches):
@@ -224,6 +250,8 @@
     scratch += [pltpu.VMEM((ncol,) + block, values.dtype) for _ in range(steps)]
     scratch += [
         pltpu.VMEM(block, jnp.float32),
+        pltpu.VMEM((rows, 1), jnp.int32),
+        pltpu.SMEM((steps,), jnp.int32),
         pltpu.VMEM((id_rows, 128), jnp.int32),
         pltpu.VMEM((n, id_rows, 128), jnp.int32),
         pltpu.VMEM((ncol, id_rows, 128), jnp.int32),
@@ -232,9 +260,9 @@
         pltpu.SemaphoreType.DMA((ncol + n - 2,)),
         pltpu.SemaphoreType.DMA((n,)),
         pltpu.SemaphoreType.DMA((ncol,)),
-        pltpu.SemaphoreType.DMA((2,)),
-        pltpu.SemaphoreType.DMA((steps, 2, n)),
-        pltpu.SemaphoreType.DMA((steps, n)),
+        pltpu.SemaphoreType.DMA((4,)),
+        pltpu.SemaphoreType.DMA((steps, 2, n, PIECES)),
+        pltpu.SemaphoreType.DMA((steps, n, PIECES)),
         pltpu.SemaphoreType.DMA((steps, ncol // 2)),
         pltpu.SemaphoreType.DMA((steps, ncol // 2)),
         pltpu.SemaphoreType.DMA((steps, ncol)),
@@ -243,7 +271,7 @@
     new = pl.pallas_call(
         functools.partial(kernel, n, ncol, steps),
         out_shape=jax.ShapeDtypeStruct(block, values.dtype),
-        in_specs=[pl.BlockSpec(memory_space=pltpu.SMEM), vmem, vmem],
+        in_specs=[pl.BlockSpec(memory_space=pl.ANY)] * 3,
         out_specs=vmem,
         scratch_shapes=scratch,
         compiler_params=pltpu.CompilerParams(

time: 58 us -> 47.1 us (0.81)
  Pallas kernels: 54.8 us -> 43.9 us
    pallas_call x1, Pallas kernels: 54.8 us -> 43.9 us  [purify(): pl.pallas_call(functools.partial(kernel, n, ncol, steps), out_shape=jax.S...]
where the time goes in v2:
time: 47.1 us; the launch traced here: 46.9 us
  Pallas kernels  43.9 us (93%)
  local copies, waits for them, and re-layouts  2.96 us (6%)
    pallas_call x1, Pallas kernels, purify(): pl.pallas_call(functools.partial(kernel, n, ncol, steps), out_shape=jax.S...  43.9 us
    unnamed x8, local copies, waits for them, and re-layouts  2.96 us

profile of v2, /device:TPU:0, one launch (start us, length us, event | category | flops | bytes accessed | tf_op | source)
XLA Modules:
  0.0 46.9 jit_solution(5451979052514391594)
XLA Ops:
  0.0 0.0 copy-start.2
  0.0 0.7 %copy-done.2 = s32[8,1]{0,1:T(1,128)S(1)} copy-done((s32[8,1]{0,1:T(1,128)S(1)}, s32[8,1]{0,1:T(1,128)}, u32[]{:S(2)}) %copy-start.2) | copy-done | bytes 56
  0.7 0.0 copy-start.1
  0.7 0.1 copy.4.ids
  0.7 0.6 %copy-done.1 = s32[2]{0:T(128)S(1)} copy-done((s32[2]{0:T(128)S(1)}, s32[2]{0:T(128)}, u32[]{:S(2)}) %copy-start.1) | copy-done | bytes 32
  1.3 0.0 copy-start
  1.3 0.9 %copy-done = bf16[8,1,128,128]{3,2,1,0:T(8,128)(2,1)S(1)} copy-done((bf16[8,1,128,128]{3,2,1,0:T(8,128)(2,1)S(1)}, bf16[8,1,128,128]{3,2,1,0:T(8,128)(2,1)}, u32[]{:S(2)}) %copy-start) | copy-done | bytes 262168
  2.3 43.9 %shard_map.37 = bf16[8,128,128]{2,1,0:T(8,128)(2,1)S(1)} custom-call(s32[2]{0:T(128)S(1)} %copy-done.1, bf16[8,128,128]{2,1,0:T(8,128)(2,1)S(1)} %bitcast.5, s32[8,1]{1,0:T(8,128)S(1)} %copy.4.ids), custom_call_target="tpu_custom_call" | custom-call | tf_op jit(solution)/shard_map/pallas_call | solution.py:271
  46.2 0.7 %copy.7 = bf16[8,1,128,128]{3,2,1,0:T(8,128)(2,1)} copy(bf16[8,1,128,128]{3,2,1,0:T(8,128)(2,1)S(1)} %bitcast.4) | data formatting | bytes 524288
Async XLA Ops:
  0.0 0.7 %copy-start.2 = (s32[8,1]{0,1:T(1,128)S(1)}, s32[8,1]{0,1:T(1,128)}, u32[]{:S(2)}) copy-start(s32[8,1]{0,1:T(1,128)} %param.4) | copy-start | bytes 100
  0.7 0.7 %copy-start.1 = (s32[2]{0:T(128)S(1)}, s32[2]{0:T(128)}, u32[]{:S(2)}) copy-start(s32[2]{0:T(128)} %branches.1) | copy-start | bytes 28
  1.3 0.9 %copy-start = (bf16[8,1,128,128]{3,2,1,0:T(8,128)(2,1)S(1)}, bf16[8,1,128,128]{3,2,1,0:T(8,128)(2,1)}, u32[]{:S(2)}) copy-start(bf16[8,1,128,128]{3,2,1,0:T(8,128)(2,1)} %param.3) | copy-start | bytes 786436

commit v3 on v2

--- a/solution.py
+++ b/solution.py
@@ -31,7 +31,7 @@
     strips, scratch = scratch[:steps], scratch[steps:]
     (acc, ids_in, branch_s, own_ids, col_ids, strip_ids, col_s, strip_s,
      id_send, id_recv_z, id_recv_c, local_sem,
-     z_send, z_recv, c_send, p_send, c_recv) = scratch
+     z_send, z_recv, c_send, p_send, d_send, c_recv) = scratch
 
     z, c = lax.axis_index("row"), lax.axis_index("col")
     chip, core = lax.div(c, 2), lax.rem(c, 2)
@@ -82,19 +82,31 @@
             bufs[step][d].at[span], bufs[step][d].at[span],
             z_send.at[step, 0, d, piece], z_recv.at[step, d, piece], (z, peer))
 
-    def c_copy(step, j):
-        src = bufs[step][0].at[0:rows]
-        return remote(src, strips[step].at[c], c_send.at[step, j], c_recv.at[step, c],
+    half = rows // 2
+
+    def c_part(step, origin, h):
+        return strips[step].at[origin, pl.ds(h * half, half)]
+
+    def c_copy(step, j, h):
+        src = bufs[step][0].at[pl.ds(h * half, half)]
+        return remote(src, c_part(step, c, h), c_send.at[step, j, h], c_recv.at[step, c, h],
                       (z, flip(chip, j) * 2 + core if j else peer))
 
-    def p_copy(step, j):
+    def pass_on(step, j, h, to):
         origin = flip(chip, j) * 2 + core
-        return remote(strips[step].at[origin], strips[step].at[origin],
-                      p_send.at[step, j], c_recv.at[step, origin], (z, peer))
-
-    def c_arrival(step, origin):
-        return remote(strips[step].at[origin], strips[step].at[origin],
-                      p_send.at[step, 0], c_recv.at[step, origin], (z, peer))
+        sem = p_send.at[step, j, h] if to == 0 else d_send.at[step, h]
+        return remote(c_part(step, origin, h), c_part(step, origin, h), sem, c_recv.at[step, origin, h],
+                      (z, flip(chip, to) * 2 + core if to else peer))
+
+    def c_arrival(step, origin, h):
+        return remote(c_part(step, origin, h), c_part(step, origin, h),
+                      p_send.at[step, 0, h], c_recv.at[step, origin, h], (z, peer))
+
+    def take_col(step, j, h):
+        c_arrival(step, flip(chip, j) * 2 + core, h).wait_recv()
+        if square and j == h + 1:
+            pass_on(step, j, h, 2 - h).start()
+        pass_on(step, j, h, 0).start()
 
     def send_own(step, piece):
         @pl.when(z > 0)
@@ -105,12 +117,15 @@
         def _():
             z_copy(step, 0, False, piece).start()
 
-    def send_col(step, js):
-        for j in js:
-            c_copy(step, j).start()
-
-    near = list(range(1, min(3, chips))) + [0]
+    square = chips == 4
+    near = list(range(1, min(3, chips)))
     far = list(range(3, chips))
+
+    def send_col(step, h):
+        for j in [0] + ([] if square else far):
+            c_copy(step, j, h).start()
+        for j in near:
+            c_copy(step, j, h).start()
 
     def add(step, d, q):
         for i in range(rows):
@@ -135,7 +150,8 @@
         copy.start()
     for piece in range(PIECES):
         send_own(0, piece)
-    send_col(0, near)
+    for h in range(2):
+        send_col(0, h)
 
     def take_ids():
         for other in col_others:
@@ -180,33 +196,35 @@
             def _():
                 add(step, n - m, z - m)
 
-        def take_col(js):
-            for j in js:
-                c_arrival(step, flip(chip, j) * 2 + core).wait_recv()
-                p_copy(step, j).start()
-
-        done = 0
-        for m in range(1, n):
+        first, second = range(PIECES // 2), range(PIECES // 2, PIECES)
+        for h, pieces in enumerate((first, second)):
+            for piece in pieces:
+                take(1, piece)
+            for j in near:
+                take_col(step, j, h)
+        if n > 2:
+            take(2, 0)
+        for h in range(2):
+            for j in far:
+                take_col(step, j, h)
+        if n > 2:
+            take(2, 1)
+        if step == 0:
+            take_ids()
+        for h in range(2):
+            for j in range(chips):
+                c_arrival(step, flip(chip, j) * 2 + 1 - core, h).wait_recv()
+        use(0)
+        if n > 2:
+            take(2, 2)
+        use(1)
+        if n > 2:
+            take(2, 3)
+            use(2)
+        for m in range(3, n):
             for piece in range(PIECES):
                 take(m, piece)
-            if m == 1:
-                send_col(step, far)
-                take_col(near[:-1])
-            if m == min(2, n - 1):
-                take_col(far)
-                if step == 0:
-                    take_ids()
-                for j in range(chips):
-                    c_arrival(step, flip(chip, j) * 2 + 1 - core).wait_recv()
-                use(0)
-                done = 1
-            if done:
-                while done < m:
-                    use(done)
-                    done += 1
-        while done < n:
-            use(done)
-            done += 1
+            use(m)
 
         branch = branch_s[step]
         for i in range(rows):
@@ -220,16 +238,19 @@
                 strips[step + 1][c, i] = new
                 if (i + 1) % part == 0:
                     send_own(step + 1, i // part)
-        if step < steps - 1:
-            send_col(step + 1, near)
+                if (i + 1) % half == 0:
+                    send_col(step + 1, i // half)
 
     for copy in sent_ids:
         copy.wait_send()
     for step in range(steps):
-        for j in range(chips):
-            c_copy(step, j).wait_send()
-            if j:
-                p_copy(step, j).wait_send()
+        for h in range(2):
+            for j in [0] + near + ([] if square else far):
+                c_copy(step, j, h).wait_send()
+            for j in range(1, chips):
+                pass_on(step, j, h, 0).wait_send()
+            if square:
+                pass_on(step, h + 1, h, 2 - h).wait_send()
         for d in range(n - 1):
             for piece in range(PIECES):
                 @pl.when((z > 0) & (z + d < n))
@@ -263,15 +284,16 @@
         pltpu.SemaphoreType.DMA((4,)),
         pltpu.SemaphoreType.DMA((steps, 2, n, PIECES)),
         pltpu.SemaphoreType.DMA((steps, n, PIECES)),
-        pltpu.SemaphoreType.DMA((steps, ncol // 2)),
-        pltpu.SemaphoreType.DMA((steps, ncol // 2)),
-        pltpu.SemaphoreType.DMA((steps, ncol)),
+        pltpu.SemaphoreType.DMA((steps, ncol // 2, 2)),
+        pltpu.SemaphoreType.DMA((steps, ncol // 2, 2)),
+        pltpu.SemaphoreType.DMA((steps, 2)),
+        pltpu.SemaphoreType.DMA((steps, ncol, 2)),
     ]
     vmem = pl.BlockSpec(memory_space=pltpu.VMEM)
     new = pl.pallas_call(
         functools.partial(kernel, n, ncol, steps),
         out_shape=jax.ShapeDtypeStruct(block, values.dtype),
-        in_specs=[pl.BlockSpec(memory_space=pl.ANY)] * 3,
+        in_specs=[pl.BlockSpec(memory_space=pltpu.HBM)] * 3,
         out_specs=vmem,
         scratch_shapes=scratch,
         compiler_params=pltpu.CompilerParams(

time: 47.1 us -> 46.3 us (0.983)
  Pallas kernels: 43.9 us -> 43.2 us
    pallas_call x1, Pallas kernels: 43.9 us -> 43.2 us  [purify(): pl.pallas_call(functools.partial(kernel, n, ncol, steps), out_shape=jax.S...]
where the time goes in v3:
time: 46.3 us; the launch traced here: 46.2 us
  Pallas kernels  43.2 us (93%)
  local copies, waits for them, and re-layouts  2.96 us (6%)
    pallas_call x1, Pallas kernels, purify(): pl.pallas_call(functools.partial(kernel, n, ncol, steps), out_shape=jax.S...  43.2 us
    unnamed x8, local copies, waits for them, and re-layouts  2.96 us

profile of v3, /device:TPU:0, one launch (start us, length us, event | category | flops | bytes accessed | tf_op | source)
XLA Modules:
  0.0 46.2 jit_solution(8753037342104135757)
XLA Ops:
  0.0 0.0 copy-start.2
  0.0 0.7 %copy-done.2 = s32[8,1]{0,1:T(1,128)S(1)} copy-done((s32[8,1]{0,1:T(1,128)S(1)}, s32[8,1]{0,1:T(1,128)}, u32[]{:S(2)}) %copy-start.2) | copy-done | bytes 56
  0.7 0.0 copy-start.1
  0.7 0.1 copy.4.ids
  0.7 0.6 %copy-done.1 = s32[2]{0:T(128)S(1)} copy-done((s32[2]{0:T(128)S(1)}, s32[2]{0:T(128)}, u32[]{:S(2)}) %copy-start.1) | copy-done | bytes 32
  1.3 0.0 copy-start
  1.3 0.9 %copy-done = bf16[8,1,128,128]{3,2,1,0:T(8,128)(2,1)S(1)} copy-done((bf16[8,1,128,128]{3,2,1,0:T(8,128)(2,1)S(1)}, bf16[8,1,128,128]{3,2,1,0:T(8,128)(2,1)}, u32[]{:S(2)}) %copy-start) | copy-done | bytes 262168
  2.3 43.2 %shard_map.37 = bf16[8,128,128]{2,1,0:T(8,128)(2,1)S(1)} custom-call(s32[2]{0:T(128)S(1)} %copy-done.1, bf16[8,128,128]{2,1,0:T(8,128)(2,1)S(1)} %bitcast.5, s32[8,1]{1,0:T(8,128)S(1)} %copy.4.ids), custom_call_target="tpu_custom_call" | custom-call | tf_op jit(solution)/shard_map/pallas_call | solution.py:293
  45.5 0.7 %copy.7 = bf16[8,1,128,128]{3,2,1,0:T(8,128)(2,1)} copy(bf16[8,1,128,128]{3,2,1,0:T(8,128)(2,1)S(1)} %bitcast.4) | data formatting | bytes 524288
Async XLA Ops:
  0.0 0.7 %copy-start.2 = (s32[8,1]{0,1:T(1,128)S(1)}, s32[8,1]{0,1:T(1,128)}, u32[]{:S(2)}) copy-start(s32[8,1]{0,1:T(1,128)} %param.4) | copy-start | bytes 100
  0.7 0.7 %copy-start.1 = (s32[2]{0:T(128)S(1)}, s32[2]{0:T(128)}, u32[]{:S(2)}) copy-start(s32[2]{0:T(128)} %branches.1) | copy-start | bytes 28
  1.3 0.9 %copy-start = (bf16[8,1,128,128]{3,2,1,0:T(8,128)(2,1)S(1)}, bf16[8,1,128,128]{3,2,1,0:T(8,128)(2,1)}, u32[]{:S(2)}) copy-start(bf16[8,1,128,128]{3,2,1,0:T(8,128)(2,1)} %param.3) | copy-start | bytes 786436

commit v4 on v3

--- a/solution.py
+++ b/solution.py
@@ -9,6 +9,7 @@
 
 BPD = 4
 PIECES = 4
+VMEM_LIMIT = 64 * 2**20 - 2**17
 MESH = pl.DeviceIdType.MESH
 
 
@@ -58,7 +59,8 @@
             bufs[step][d][rows] = jnp.zeros(values.shape[1:], values.dtype)
     for load in loads:
         load.wait()
-    own_ids[0:rows, :] = jnp.broadcast_to(ids_in[...], (rows, own_ids.shape[1]))
+    for i in range(rows):
+        own_ids[i] = jnp.full(own_ids.shape[1:], ids_in[i], jnp.int32)
     strip_ids[c] = own_ids[...]
     col_ids[z] = own_ids[...]
     pl.semaphore_wait(barrier, ncol + n - 2)
@@ -271,7 +273,7 @@
     scratch += [pltpu.VMEM((ncol,) + block, values.dtype) for _ in range(steps)]
     scratch += [
         pltpu.VMEM(block, jnp.float32),
-        pltpu.VMEM((rows, 1), jnp.int32),
+        pltpu.SMEM((rows,), jnp.int32),
         pltpu.SMEM((steps,), jnp.int32),
         pltpu.VMEM((id_rows, 128), jnp.int32),
         pltpu.VMEM((n, id_rows, 128), jnp.int32),
@@ -297,8 +299,8 @@
         out_specs=vmem,
         scratch_shapes=scratch,
         compiler_params=pltpu.CompilerParams(
-            collective_id=0, has_side_effects=True, vmem_limit_bytes=48 * 2**20),
-    )(branches, values.reshape(block), column_slot_index)
+            collective_id=0, has_side_effects=True, vmem_limit_bytes=VMEM_LIMIT),
+    )(branches, values.reshape(block), column_slot_index.reshape(rows))
     return new.reshape(values.shape)
 
 

time: 46.3 us -> 45.6 us (0.985)
  local copies, waits for them, and re-layouts: 2.96 us -> 1.67 us
  Pallas kernels: 43.2 us -> 43.8 us
    unnamed x8 -> x1, local copies, waits for them, and re-layouts: 2.96 us -> 1.67 us
    pallas_call x1, Pallas kernels: 43.2 us -> 43.8 us  [purify(): pl.pallas_call(functools.partial(kernel, n, ncol, steps), out_shape=jax.S...]
where the time goes in v4:
time: 45.6 us; the launch traced here: 45.5 us
  Pallas kernels  43.8 us (96%)
  local copies, waits for them, and re-layouts  1.67 us (4%)
    pallas_call x1, Pallas kernels, purify(): pl.pallas_call(functools.partial(kernel, n, ncol, steps), out_shape=jax.S...  43.8 us
    unnamed x1, local copies, waits for them, and re-layouts  1.67 us

profile of v4, /device:TPU:0, one launch (start us, length us, event | category | flops | bytes accessed | tf_op | source)
XLA Modules:
  0.0 45.5 jit_solution(15930461908173728607)
XLA Ops:
  0.0 43.8 %shard_map.37 = bf16[8,128,128]{2,1,0:T(8,128)(2,1)} custom-call(s32[2]{0:T(128)} %branches.1, bf16[8,128,128]{2,1,0:T(8,128)(2,1)} %bitcast.6, s32[8]{0:T(128)} %bitcast.7), custom_call_target="tpu_custom_call" | custom-call | tf_op jit(solution)/shard_map/pallas_call | solution.py:295
  43.8 1.7 %copy.6 = bf16[8,1,128,128]{3,2,1,0:T(8,128)(2,1)} copy(bf16[8,1,128,128]{3,2,1,0:T(8,128)(2,1)} %bitcast.5) | data formatting | bytes 524288

commit v5 on v4

--- a/solution.py
+++ b/solution.py
@@ -9,7 +9,7 @@
 
 BPD = 4
 PIECES = 4
-VMEM_LIMIT = 64 * 2**20 - 2**17
+VMEM_LIMIT = 64 * 2**20 - 2**17 - 2**18
 MESH = pl.DeviceIdType.MESH
 
 
@@ -27,8 +27,8 @@
     per = rows // BPD
     part = rows // PIECES
     chips = ncol // 2
-    bufs = [scratch[s * n:(s + 1) * n] for s in range(steps)]
-    scratch = scratch[steps * n:]
+    bufs = [[scratch[(s * n + d) * per:(s * n + d + 1) * per] for d in range(n)] for s in range(steps)]
+    scratch = scratch[steps * n * per:]
     strips, scratch = scratch[:steps], scratch[steps:]
     (acc, ids_in, branch_s, own_ids, col_ids, strip_ids, col_s, strip_s,
      id_send, id_recv_z, id_recv_c, local_sem,
@@ -38,8 +38,13 @@
     chip, core = lax.div(c, 2), lax.rem(c, 2)
     peer = c + 1 - 2 * core
 
+    def blocks(step, d, start, size):
+        return bufs[step][d][start // BPD].at[pl.ds(start % BPD, size)]
+
     loads = [
-        pltpu.make_async_copy(values, bufs[0][0].at[0:rows], local_sem.at[0]),
+        pltpu.make_async_copy(values.at[pl.ds(t * BPD, BPD)], bufs[0][0][t].at[0:BPD], local_sem.at[4 + t])
+        for t in range(per)
+    ] + [
         pltpu.make_async_copy(values, strips[0].at[c], local_sem.at[1]),
         pltpu.make_async_copy(ids, ids_in, local_sem.at[2]),
         pltpu.make_async_copy(branches, branch_s, local_sem.at[3]),
@@ -56,7 +61,8 @@
     own_ids[...] = jnp.zeros_like(own_ids)
     for step in range(steps):
         for d in range(n):
-            bufs[step][d][rows] = jnp.zeros(values.shape[1:], values.dtype)
+            for t in range(per):
+                bufs[step][d][t][BPD] = jnp.zeros(values.shape[1:], values.dtype)
     for load in loads:
         load.wait()
     for i in range(rows):
@@ -72,16 +78,15 @@
 
     def z_copy(step, d, down, piece):
         at = d + 1 if down else (d - 1) % n
-        span = pl.ds(piece * part, part)
         return remote(
-            bufs[step][d].at[span], bufs[step][at].at[span],
+            blocks(step, d, piece * part, part), blocks(step, at, piece * part, part),
             z_send.at[step, 0 if down else 1, d, piece], z_recv.at[step, at, piece],
             (jnp.maximum(z - 1, 0) if down else jnp.minimum(z + 1, n - 1), c))
 
     def z_arrival(step, d, piece):
-        span = pl.ds(piece * part, part)
+        span = blocks(step, d, piece * part, part)
         return remote(
-            bufs[step][d].at[span], bufs[step][d].at[span],
+            span, span,
             z_send.at[step, 0, d, piece], z_recv.at[step, d, piece], (z, peer))
 
     half = rows // 2
@@ -90,7 +95,7 @@
         return strips[step].at[origin, pl.ds(h * half, half)]
 
     def c_copy(step, j, h):
-        src = bufs[step][0].at[pl.ds(h * half, half)]
+        src = blocks(step, 0, h * half, half)
         return remote(src, c_part(step, c, h), c_send.at[step, j, h], c_recv.at[step, c, h],
                       (z, flip(chip, j) * 2 + core if j else peer))
 
@@ -129,16 +134,15 @@
         for j in near:
             c_copy(step, j, h).start()
 
-    def add(step, d, q):
+    def add(step, d, q, ts):
         for i in range(rows):
             left, right = [], []
-            for t in range(per):
+            for t in ts:
                 p = q * per + t
-                slot = strip_s[p, i, 0]
-                k = t * BPD + slot
-                k = jnp.where(col_s[q, k, 0] == col_s[z, i, 0], k, rows)
+                k = strip_s[p, i, 0]
+                k = jnp.where(col_s[q, t * BPD + k, 0] == col_s[z, i, 0], k, BPD)
                 left.append(strips[step][p, i])
-                right.append(bufs[step][d][k])
+                right.append(bufs[step][d][t][k])
             term = jnp.dot(jnp.concatenate(left, 1), jnp.concatenate(right, 0),
                            preferred_element_type=jnp.float32)
             acc[i] = term if d == 0 else acc[i] + term
@@ -185,18 +189,18 @@
                     def _():
                         z_copy(step, n - m, False, piece).start()
 
-        def use(m):
+        def use(m, ts=range(per)):
             if m == 0:
-                add(step, 0, z)
+                add(step, 0, z, ts)
                 return
 
             @pl.when(z + m < n)
             def _():
-                add(step, m, z + m)
+                add(step, m, z + m, ts)
 
             @pl.when(z - m >= 0)
             def _():
-                add(step, n - m, z - m)
+                add(step, n - m, z - m, ts)
 
         first, second = range(PIECES // 2), range(PIECES // 2, PIECES)
         for h, pieces in enumerate((first, second)):
@@ -224,19 +228,23 @@
             take(2, 3)
             use(2)
         for m in range(3, n):
-            for piece in range(PIECES):
-                take(m, piece)
-            use(m)
+            for t in range(per):
+                for piece in range(t * PIECES // per, (t + 1) * PIECES // per):
+                    take(m, piece)
+                if m == n - 1:
+                    use(m, [t])
+            if m < n - 1:
+                use(m)
 
         branch = branch_s[step]
         for i in range(rows):
-            old = bufs[step][0][i].astype(jnp.float32)
+            old = bufs[step][0][i // BPD][i % BPD].astype(jnp.float32)
             total = acc[i]
             new = jnp.where(branch == 1, 2.0 * old - total, total).astype(values.dtype)
             if step == steps - 1:
                 out[i] = new
             else:
-                bufs[step + 1][0][i] = new
+                bufs[step + 1][0][i // BPD][i % BPD] = new
                 strips[step + 1][c, i] = new
                 if (i + 1) % part == 0:
                     send_own(step + 1, i // part)
@@ -269,7 +277,7 @@
     steps = branches.shape[0]
     block = (rows, bs, bs)
     id_rows = -(-rows // 8) * 8
-    scratch = [pltpu.VMEM((rows + 1, bs, bs), values.dtype) for _ in range(steps * n)]
+    scratch = [pltpu.VMEM((BPD + 1, bs, bs), values.dtype) for _ in range(steps * n * (rows // BPD))]
     scratch += [pltpu.VMEM((ncol,) + block, values.dtype) for _ in range(steps)]
     scratch += [
         pltpu.VMEM(block, jnp.float32),
@@ -283,7 +291,7 @@
         pltpu.SemaphoreType.DMA((ncol + n - 2,)),
         pltpu.SemaphoreType.DMA((n,)),
         pltpu.SemaphoreType.DMA((ncol,)),
-        pltpu.SemaphoreType.DMA((4,)),
+        pltpu.SemaphoreType.DMA((4 + rows // BPD,)),
         pltpu.SemaphoreType.DMA((steps, 2, n, PIECES)),
         pltpu.SemaphoreType.DMA((steps, n, PIECES)),
         pltpu.SemaphoreType.DMA((steps, ncol // 2, 2)),
@@ -294,7 +302,7 @@
     vmem = pl.BlockSpec(memory_space=pltpu.VMEM)
     new = pl.pallas_call(
         functools.partial(kernel, n, ncol, steps),
-        out_shape=jax.ShapeDtypeStruct(block, values.dtype),
+        out_shape=pltpu.VMEM(block, values.dtype),
         in_specs=[pl.BlockSpec(memory_space=pltpu.HBM)] * 3,
         out_specs=vmem,
         scratch_shapes=scratch,

time: 45.6 us -> 44 us (0.965)
  local copies, waits for them, and re-layouts: 1.67 us -> 0.71 us
  Pallas kernels: 43.8 us -> 43.1 us
    unnamed x1, local copies, waits for them, and re-layouts: 1.67 us -> 0.71 us
    pallas_call x1, Pallas kernels: 43.8 us -> 43.1 us  [purify(): pl.pallas_call(functools.partial(kernel, n, ncol, steps), out_shape=pltpu...]
where the time goes in v5:
time: 44 us; the launch traced here: 43.8 us
  Pallas kernels  43.1 us (98%)
  local copies, waits for them, and re-layouts  0.71 us (2%)
    pallas_call x1, Pallas kernels, purify(): pl.pallas_call(functools.partial(kernel, n, ncol, steps), out_shape=pltpu...  43.1 us

profile of v5, /device:TPU:0, one launch (start us, length us, event | category | flops | bytes accessed | tf_op | source)
XLA Modules:
  0.0 43.8 jit_solution(8936658252601205390)
XLA Ops:
  0.0 43.1 %shard_map.37 = bf16[8,128,128]{2,1,0:T(8,128)(2,1)S(1)} custom-call(s32[2]{0:T(128)} %branches.1, bf16[8,128,128]{2,1,0:T(8,128)(2,1)} %bitcast.6, s32[8]{0:T(128)} %bitcast.7), custom_call_target="tpu_custom_call" | custom-call | tf_op jit(solution)/shard_map/pallas_call | solution.py:303
  43.1 0.7 %copy.6 = bf16[8,1,128,128]{3,2,1,0:T(8,128)(2,1)} copy(bf16[8,1,128,128]{3,2,1,0:T(8,128)(2,1)S(1)} %bitcast.5) | data formatting | bytes 524288
